TPU v7x, 128 devices: a whole 4x4x4 slice. The times are simulated.
128 devices in a mesh: head: 4 (over x), frame: 32 (over y, z, core).
Axes of the slice: x: 4, y: 4, z: 4, core: 2. Of those that a mesh axis runs over, the one named last changes fastest.
Arguments:
- frames_x: bfloat16 [16384, 3072], P('frame'), may hold values from -6 to 6
- w_qkv: bfloat16 [3072, 9216], P(None, 'head'), may hold values from -0.109375 to 0.109375
- q_gain: float32 [128], replicated, may hold values from 0.5 to 2.5
- k_gain: float32 [128], replicated, may hold values from 0.5 to 2.5
- head_kind: int32 [24], P('head'), may hold values from 0 to 1, as said below
- w_out: bfloat16 [3072, 3072], P('head'), may hold values from -0.109375 to 0.109375
Outputs:
- mixed: bfloat16 [16384, 3072], P('frame', 'head')
Inputs may be any that keep to these rules, and one draw needn't show every extreme that they name: `head_kind`: in each group of 6 consecutive heads, 1 to 4 heads are temporal; some group has exactly 4.
All inputs are finite; a program needn't handle non-finite values.
Results may differ from a plain program's by a relative error of at most 0.015.
Values may be sent and summed in bfloat16 or wider, within the bound.
A program may use at most 192 MiB of HBM per device.

v0:
```python
import math

import jax
import jax.numpy as jnp
from jax import lax
from jax.sharding import PartitionSpec as P

TMAX = 4


EPSILON = 1e-06


def from_root(block, axis, holder):
    block = jnp.where(lax.axis_index(axis) == holder, block, jnp.zeros_like(block))
    return lax.psum(block, axis)


def rms_norm(values, gains):
    mean_square = jnp.mean(values * values, axis=-1, keepdims=True)
    return values * lax.rsqrt(mean_square + EPSILON) * gains


def softmax_rows(scores):
    shifted = scores - jnp.max(scores, axis=-1, keepdims=True)
    weights = jnp.exp(shifted)
    return weights / jnp.sum(weights, axis=-1, keepdims=True)


def per_device(frames_x, w_qkv, q_gain, k_gain, head_kind, w_out):
    tok_rows = frames_x.shape[0]
    per_group = head_kind.shape[0]
    head_dim = q_gain.shape[0]
    scale = 1.0 / math.sqrt(head_dim)
    projected = jnp.dot(frames_x, w_qkv, preferred_element_type=jnp.float32)
    projected = projected.reshape(tok_rows, per_group, 3, head_dim)
    queries = rms_norm(projected[:, :, 0], q_gain).astype(jnp.bfloat16)
    keys = rms_norm(projected[:, :, 1], k_gain).astype(jnp.bfloat16)
    values = projected[:, :, 2].astype(jnp.bfloat16)
    stacked = jnp.concatenate([queries, keys, values], axis=-1).transpose(1, 0, 2)
    positions = jnp.arange(per_group, dtype=jnp.int32)
    order = jnp.argsort((1 - head_kind) * per_group + positions)
    temporal_slots = order[:TMAX]
    spatial_slots = order[1:]
    temporal_valid = head_kind[temporal_slots] == 1
    spatial_valid = head_kind[spatial_slots] == 0
    temporal_in = jnp.take(stacked, temporal_slots, axis=0)
    spatial_in = jnp.take(stacked, spatial_slots, axis=0)
    remote = lax.all_gather(temporal_in[:, :, head_dim:], "frame", axis=1, tiled=True)
    remote = remote.reshape(TMAX, -1, tok_rows, 2 * head_dim)
    scores = (
        jnp.einsum(
            "std,sftd->stf",
            temporal_in[:, :, :head_dim],
            remote[..., :head_dim],
            preferred_element_type=jnp.float32,
        )
        * scale
    )
    probs = softmax_rows(scores).astype(jnp.bfloat16)
    temporal_out = jnp.einsum(
        "stf,sftd->std", probs, remote[..., head_dim:], preferred_element_type=jnp.float32
    ).astype(jnp.bfloat16)
    own_pairs = spatial_in[:, :, head_dim:]
    first_pairs = from_root(own_pairs, "frame", 0)
    wide = jnp.concatenate([own_pairs, first_pairs], axis=1)
    spatial_scores = (
        jnp.einsum(
            "std,sud->stu",
            spatial_in[:, :, :head_dim],
            wide[..., :head_dim],
            preferred_element_type=jnp.float32,
        )
        * scale
    )
    spatial_probs = softmax_rows(spatial_scores).astype(jnp.bfloat16)
    spatial_out = jnp.einsum(
        "stu,sud->std", spatial_probs, wide[..., head_dim:], preferred_element_type=jnp.float32
    ).astype(jnp.bfloat16)
    temporal_pick = (
        (temporal_slots[:, None] == positions[None, :]) & temporal_valid[:, None]
    ).astype(jnp.bfloat16)
    spatial_pick = ((spatial_slots[:, None] == positions[None, :]) & spatial_valid[:, None]).astype(
        jnp.bfloat16
    )
    heads = jnp.einsum(
        "sh,std->thd", temporal_pick, temporal_out, preferred_element_type=jnp.float32
    )
    heads = heads + jnp.einsum(
        "sh,std->thd", spatial_pick, spatial_out, preferred_element_type=jnp.float32
    )
    attention = heads.astype(jnp.bfloat16).reshape(tok_rows, per_group * head_dim)
    group_part = jnp.dot(attention, w_out, preferred_element_type=jnp.float32).astype(jnp.bfloat16)
    group_part = lax.optimization_barrier(group_part).astype(jnp.float32)
    total = lax.psum_scatter(
        group_part.astype(jnp.bfloat16), "head", scatter_dimension=1, tiled=True
    )
    return total


def solution(mesh):
    placed = (P("frame", None), P(None, "head"), P(), P(), P("head"), P("head", None))
    return jax.shard_map(
        per_device, mesh=mesh, in_specs=placed, out_specs=P("frame", "head"), check_vma=False
    )
```

profile of v0, /device:TPU:0, one launch (start us, length us, event | category | flops | bytes accessed | tf_op | source)
XLA Modules:
  0.0 376.1 jit_solution(2648682336664070681)
XLA Ops:
  6.5 0.0 copy-start
  6.5 0.0 all-reduce.2.cloned.1.call-start
  6.5 1.9 copy-done
  8.4 10.3 %fusion.59 = f32[512,2304]{0,1:T(8,128)S(1)} fusion(bf16[512,3072]{1,0:T(8,128)(2,1)S(1)} %copy-done, bf16[3072,2304]{1,0:T(8,128)(2,1)} %param.7), kind=kOutput, calls=%fused_computation.86 | convolution fusion | flops 7247757312 | bytes 22020096 | tf_op jit(solution)/shard_map/dot_general | solution.py:35
  18.7 0.1 slice.87
  18.8 0.0 copy-start.2
  18.9 2.2 fusion.57
  21.1 0.0 copy-done.2
  21.1 1.0 sort.17
  22.1 0.1 compare_and_fusion
  22.1 1.9 copy.27
  24.0 1.2 copy.17
  25.2 0.5 fusion.15
  25.7 0.0 copy-start.8
  25.7 0.0 copy-start.9
  25.7 3.0 copy.28
  28.7 1.9 fusion.12
  30.6 0.0 copy-done.8
  30.7 0.0 copy-done.9
  30.7 0.0 copy-start.5
  30.7 2.2 fusion.14
  32.9 0.0 copy-done.5
  32.9 0.3 maximum_bitcast_fusion
  33.2 2.3 gather_fusion.2
  35.5 1.8 broadcast_select_fusion
  37.4 0.0 copy-start.3
  37.4 1.3 copy-done.3
  38.6 1.6 broadcast_select_fusion.2
  40.3 0.0 all-reduce.2.cloned.1.call-update
  40.3 0.0 all-gather.2.cloned.1.call-start
  40.4 1.9 gather_fusion
  42.3 1.7 broadcast_select_fusion.1
  44.0 0.0 copy-start.4
  44.0 1.1 slice.65
  45.0 0.0 all-gather.2.cloned.1.call-update
  45.1 0.0 reduce-scatter.2.cloned.1.call-start
  45.1 0.1 slice.48
  45.2 0.6 gather_fusion.3
  45.8 0.6 gather_fusion.1
  46.5 0.9 slice_bitcast_fusion
  47.4 100.9 %all-reduce.2.cloned.1.call-done = bf16[5,512,256]{2,1,0:T(8,128)(2,1)} async-done(((bf16[5,512,256]{2,1,0:T(8,128)(2,1)}), bf16[5,512,256]{2,1,0:T(8,128)(2,1)}) %all-reduce.2.cloned.1.call-update) | async-done | bytes 1310736 | tf_op jit(solution)/shard_map/psum | solution.py:16
  148.3 0.0 copy-done.4
  148.3 6.8 %fusion.21 = f32[5,512,1024]{2,1,0:T(8,128)} fusion(bf16[5,512,256]{2,1,0:T(8,128)(2,1)S(1)} %copy-done.4, bf16[5,512,256]{2,1,0:T(8,128)(2,1)} %all-reduce.2.cloned.1.call-done, bf16[5,512,384]{2,1,0:T(8,128)(2,1)} %copy-done.3), kind=kOutput, calls=%fused_computation.38 | convolution fusion | flops 673710080 | bytes 13762560 | tf_op jit(solution)/shard_map/std,sud->stu/dot_general | solution.py:68
  155.0 0.0 copy-start.6
  155.0 10.8 %fusion.58 = f32[5,512]{1,0:T(8,128)S(1)} fusion(f32[5,512,1024]{2,1,0:T(8,128)} %fusion.21), kind=kOutput, calls=%fused_computation.85 | output fusion | flops 10486783 | bytes 10496000 | tf_op jit(solution)/shard_map/sub | solution.py:25
  165.8 0.0 copy-done.6
  165.8 11.0 %fusion.19 = bf16[5,512,128]{2,1,0:T(8,128)(2,1)} fusion(f32[5,512]{1,0:T(8,128)S(1)} %fusion.58, bf16[5,512,256]{2,1,0:T(8,128)(2,1)S(1)} %copy-done.6, bf16[5,512,256]{2,1,0:T(8,128)(2,1)S(1)} %copy-done.4, f32[5,512,1024]{2,1,0:T(8,128)} %fusion.21), kind=kOutput, calls=%fused_computation.36 | convolution fusion | flops 687148544 | bytes 13772800 | tf_op jit(solution)/shard_map/stu,sud->std/dot_general | solution.py:77
  176.8 1.6 fusion.30
  178.4 85.8 %all-gather.2.cloned.1.call-done = bf16[4,16384,256]{2,1,0:T(8,128)(2,1)} async-done(((bf16[4,512,256]{2,1,0:T(8,128)(2,1)}), bf16[4,16384,256]{2,1,0:T(8,128)(2,1)}) %all-gather.2.cloned.1.call-update) | async-done | bytes 33554448 | tf_op jit(solution)/shard_map/all_gather | solution.py:49
  264.2 0.0 copy-start.7
  264.2 23.1 %fusion.56 = (bf16[4,32,512,128]{3,2,1,0:T(8,128)(2,1)}, bf16[4,32,512,128]{3,2,1,0:T(8,128)(2,1)}) fusion(bf16[4,32,512,256]{3,2,1,0:T(8,128)(2,1)} %bitcast.52), kind=kLoop, calls=%fused_computation.83 | loop fusion | bytes 67108864 | tf_op jit(solution)/shard_map/slice | solution.py:62
  287.2 0.0 copy-done.7
  287.2 16.9 %fusion.5 = f32[4,512,1,32]{3,2,1,0:T(1,128)S(1)} fusion(bf16[4,32,512,128]{3,2,1,0:T(8,128)(2,1)} %get-tuple-element.12, bf16[4,512,128,1]{2,1,0,3:T(8,128)(2,1)S(1)} %copy-done.7), kind=kOutput, calls=%fused_computation.9 | convolution fusion | flops 16777216 | bytes 17563648 | tf_op jit(solution)/shard_map/std,sftd->stf/dot_general | solution.py:52
  304.2 0.5 copy.23
  304.7 0.1 fusion.28
  304.8 0.7 copy.24
  305.6 17.1 %fusion.3 = bf16[4,512,1,128]{3,2,1,0:T(2,128)(2,1)S(1)} fusion(bf16[4,512,32,1]{2,3,1,0:T(2,128)(2,1)S(1)} %copy.24, bf16[4,32,512,128]{3,2,1,0:T(8,128)(2,1)} %get-tuple-element.11), kind=kOutput, calls=%fused_computation.7 | convolution fusion | flops 16777216 | bytes 17432576 | tf_op jit(solution)/shard_map/stf,sftd->std/dot_general | solution.py:61
  322.6 0.9 fusion.18
  323.6 1.3 copy.19
  324.9 0.0 copy-start.1
  324.9 7.0 %convolution_convert_fusion = bf16[512,3072]{1,0:T(8,128)(2,1)} fusion(bf16[512,768]{0,1:T(8,128)(2,1)} %bitcast.56, bf16[768,3072]{1,0:T(8,128)(2,1)} %param.11), kind=kOutput, calls=%fused_computation.17 | convolution fusion | flops 2417491968 | bytes 8650752 | tf_op jit(solution)/shard_map/dot_general | solution.py:93
  331.9 0.0 reduce-scatter.2.cloned.1.call-update
  332.0 37.6 %reduce-scatter.2.cloned.1.call-done = bf16[512,768]{1,0:T(8,128)(2,1)} async-done(((bf16[512,3072]{1,0:T(8,128)(2,1)}), bf16[512,768]{1,0:T(8,128)(2,1)}) %reduce-scatter.2.cloned.1.call-update) | async-done | bytes 786448 | tf_op jit(solution)/shard_map/reduce_scatter | solution.py:95
  369.6 0.0 copy-done.1
  (9 shorter events, 0.1 us)
Async XLA Ops:
  6.5 1.9 copy-start
  6.5 141.7 %all-reduce.2.cloned.1.call-start = ((), (), s32[]{:S(2)}) async-start(), calls=%async_computation.2 | async-start | bytes 2621440 | tf_op jit(solution)/shard_map/psum | solution.py:16
  18.8 2.2 copy-start.2
  25.7 5.0 %copy-start.8 = (f32[128]{0:T(128)S(1)}, f32[128]{0:T(128)}, u32[]{:S(2)}) copy-start(f32[128]{0:T(128)} %param.9) | copy-start | bytes 1540
  25.7 5.0 %copy-start.9 = (f32[128]{0:T(128)S(1)}, f32[128]{0:T(128)}, u32[]{:S(2)}) copy-start(f32[128]{0:T(128)} %param.8) | copy-start | bytes 1540
  30.7 2.2 copy-start.5
  37.4 1.3 copy-start.3
  40.3 223.9 %all-gather.2.cloned.1.call-start = ((), (), s32[]{:S(2)}) async-start(), calls=%async_computation.1 | async-start | bytes 34603008 | tf_op jit(solution)/shard_map/all_gather | solution.py:49
  44.0 104.3 %copy-start.4 = (bf16[5,512,256]{2,1,0:T(8,128)(2,1)S(1)}, bf16[5,512,256]{2,1,0:T(8,128)(2,1)}, u32[]{:S(2)}) copy-start(bf16[5,512,256]{2,1,0:T(8,128)(2,1)} %get-tuple-element.16) | copy-start | bytes 3932164
  45.1 324.5 %reduce-scatter.2.cloned.1.call-start = ((), (), s32[]{:S(2)}) async-start(), calls=%async_computation.3 | async-start | bytes 3932160 | tf_op jit(solution)/shard_map/reduce_scatter | solution.py:95
  155.0 10.8 %copy-start.6 = (bf16[5,512,256]{2,1,0:T(8,128)(2,1)S(1)}, bf16[5,512,256]{2,1,0:T(8,128)(2,1)}, u32[]{:S(2)}) copy-start(bf16[5,512,256]{2,1,0:T(8,128)(2,1)} %all-reduce.2.cloned.1.call-done) | copy-start | bytes 3932164
  264.2 23.1 %copy-start.7 = (bf16[4,512,128,1]{2,1,0,3:T(8,128)(2,1)S(1)}, bf16[4,512,128,1]{2,1,0,3:T(8,128)(2,1)}, u32[]{:S(2)}) copy-start(bf16[4,512,128,1]{2,1,0,3:T(8,128)(2,1)} %slice_bitcast_fusion) | copy-start | bytes 1572868
  324.9 44.7 %copy-start.1 = (bf16[512,3072]{1,0:T(8,128)(2,1)S(1)}, bf16[512,3072]{1,0:T(8,128)(2,1)}, u32[]{:S(2)}) copy-start(bf16[512,3072]{1,0:T(8,128)(2,1)} %param.6) | copy-start | bytes 9437188
Sparse Core Ops, SparseCore 0:
  40.4 107.8 all-reduce.1
  150.6 113.4 all-gather.1
  332.1 37.4 reduce-scatter.1
where the time goes:
time: 377 us; the launch traced here: 376 us
  waiting for transfers between devices  224 us (59%)
  matrix products  71.6 us (19%)
  local copies, waits for them, and re-layouts  44.8 us (12%)
  other arithmetic  22 us (6%)
  between operations  13.3 us (4%)
    psum x1, waiting for transfers between devices, from_root(): return lax.psum(block, axis)  101 us
    all_gather x1, waiting for transfers between devices, per_device(): lax.all_gather(temporal_in[:, :, head_dim:], 'frame', axis=1, tiled=True)  85.8 us
    reduce_scatter x1, waiting for transfers between devices, per_device(): lax.psum_scatter(group_part.astype(jnp.bfloat16), 'head', scatter_dimensi...  37.6 us
    slice x1, local copies, waits for them, and re-layouts, per_device(): remote[..., head_dim:]  23.1 us
    dot_general x1, matrix products, per_device(): jnp.einsum('stf,sftd->std', probs, remote[..., head_dim:], preferred_elem...  17.1 us
    dot_general x1, matrix products, per_device(): jnp.einsum('std,sftd->stf', temporal_in[:, :, :head_dim], remote[..., :he...  16.9 us
    dot_general x1, matrix products, per_device(): jnp.einsum('stu,sud->std', spatial_probs, wide[..., head_dim:], preferred...  11 us
    sub x1, other arithmetic, softmax_rows(): shifted = scores - jnp.max(scores, axis=-1, keepdims=True)  10.8 us
  transfers between devices with their start and end apart: 3, of which 3 were waited for; matrix products, arithmetic and copies ran while one was open for 10% of the time, Pallas kernels for 0%

commit v1 on v0

v1 whole, which is shorter than its diff:
```python
import functools
import math

import jax
import jax.numpy as jnp
from jax import lax
from jax.experimental import pallas as pl
from jax.experimental.pallas import tpu as pltpu
from jax.sharding import PartitionSpec as P

MESH = pl.DeviceIdType.MESH
EPSILON = 1e-06
HPG = 6
TMAX = 4
HD = 128
TOK = 512
D = 3072
WAVES = 4
WT = TOK // WAVES
COLS = D // 4
HALF = WT // 2
BF = jnp.bfloat16
F32 = jnp.float32


def dot(a, b):
    return jnp.dot(a, b, preferred_element_type=F32)


def dot_t(a, b):
    return lax.dot_general(a, b, (((1,), (1,)), ((), ())), preferred_element_type=F32)


def arrived(ref, sem):
    pltpu.make_async_copy(ref, ref, sem).wait()


def kernel(
    kinds, x_hbm, w_hbm, qg_ref, kg_ref, wo_hbm, out_ref,
    x, w, wo, qkv, kv0, sbuf, rbuf, obuf, tbuf, perm, unperm, sp, att,
    far_s, far_r, near_s, near_r,
    load_sem, a2a_s, a2a_r, ret_s, ret_r, sc_s, sc_r, st_s, st_r, fs_sem, fr_sem, ns_sem, nr_sem,
):
    nf = 32
    h = lax.axis_index("head")
    f = lax.axis_index("frame")
    core = lax.rem(f, 2)
    chip = f // 2
    y, z = chip // 4, lax.rem(chip, 4)
    left, right, opposite = lax.rem(h + 3, 4), lax.rem(h + 1, 4), lax.rem(h + 2, 4)

    barrier = pltpu.get_barrier_semaphore()

    @pl.loop(1, nf)
    def _(i):
        pl.semaphore_signal(barrier, inc=1, device_id=(h, lax.rem(f + i, nf)), device_id_type=MESH)

    for peer in (left, right):
        pl.semaphore_signal(barrier, inc=1, device_id=(peer, f), device_id_type=MESH)

    loads = [pltpu.make_async_copy(x_hbm, x, load_sem.at[0])]
    for c in range(3):
        loads.append(
            pltpu.make_async_copy(w_hbm.at[:, pl.ds(768 * c, 768)], w.at[c], load_sem.at[1 + c])
        )
    for b in range(4):
        loads.append(
            pltpu.make_async_copy(wo_hbm.at[:, pl.ds(COLS * b, COLS)], wo.at[b], load_sem.at[4 + b])
        )
    for load in loads:
        load.start()

    kind = [kinds[j] for j in range(HPG)]
    count = sum(kind)
    holds = [[None] * HPG for _ in range(TMAX)]
    before = jnp.int32(0)
    for j in range(HPG):
        rank = kind[j] * before + (1 - kind[j]) * (count + j - before)
        for t in range(TMAX):
            holds[t][j] = (1 - jnp.minimum((rank - t) * (rank - t), 1)).astype(F32)
        before = before + kind[j]
    kind = [val.astype(F32) for val in kind]

    def spread(shape, mixed_dim):
        mixed = lax.broadcasted_iota(jnp.int32, shape, mixed_dim)
        token = lax.broadcasted_iota(jnp.int32, shape, 1 - mixed_dim)
        same = ((mixed // 16) * 4 + mixed % 4 == token).astype(F32)
        slot = (mixed // 4) % 4
        return [jnp.where(slot == t, same, 0.0) for t in range(TMAX)]

    slots = spread((TOK, WT), 0)
    for j in range(HPG):
        perm[:, WT * j : WT * j + WT] = sum(slots[t] * holds[t][j] for t in range(TMAX)).astype(BF)
    slots = spread((WT, TOK), 1)
    for j in range(HPG):
        total = sum(slots[t] * (holds[t][j] * kind[j]) for t in range(TMAX))
        unperm[WT * j : WT * j + WT] = total.astype(BF)
    for j in range(HPG):
        qkv[j, :, 3 * HD :] = jnp.ones((TOK, HD), BF)
        kv0[j, :, 2 * HD :] = jnp.ones((TOK, HD), BF)
    for v in range(WAVES):
        rbuf[v, :, 3 * HD :] = jnp.ones((TOK, HD), BF)

    q_gain = qg_ref[...] * (math.log2(math.e) / math.sqrt(HD))
    k_gain = kg_ref[...]

    def norm(val, gain):
        mean_square = jnp.mean(val * val, axis=-1, keepdims=True)
        return (val * lax.rsqrt(mean_square + EPSILON) * gain).astype(BF)

    def project(c):
        loads[1 + c].wait()
        for part in range(3):
            val = dot(x[...], w[c, :, 256 * part : 256 * part + 256])
            for side in range(2):
                piece = 2 * part + side
                head, role = 2 * c + piece // 3, piece % 3
                block = val[:, HD * side : HD * side + HD]
                if role == 0:
                    block = norm(block, q_gain)
                elif role == 1:
                    block = norm(block, k_gain)
                else:
                    block = block.astype(BF)
                qkv[head, :, HD * role : HD * role + HD] = block

    batches = ((0, 4, True), (4, 2, False))

    def cut(batch, start, size):
        lo, n, _ = batches[batch]
        return kv0.at[pl.ds(lo, n), pl.ds(start, size), pl.ds(0, 2 * HD)]

    def device_of(yy, zz):
        return (yy * 4 + zz) * 2

    def scatter(batch):
        lo, n, z_first = batches[batch]

        @pl.when(f == 0)
        def _():
            kv0[lo : lo + n, :, : 2 * HD] = qkv[lo : lo + n, :, HD : 3 * HD]

            @pl.loop(1, 16)
            def _(q):
                major, minor = q // 4, lax.rem(q, 4)
                target = device_of(major, minor) if z_first else device_of(minor, major)
                piece = cut(batch, pl.multiple_of(q * 32, 32), 32)
                pltpu.make_async_remote_copy(
                    src_ref=piece, dst_ref=piece, send_sem=sc_s.at[batch], recv_sem=sc_r.at[batch],
                    device_id=(h, target), device_id_type=MESH,
                ).start()

    def peers_copy(batch, stage, start, size, along_z):
        for i in range(1, 4):
            if along_z:
                target = device_of(y, lax.rem(z + i, 4))
            else:
                target = device_of(lax.rem(y + i, 4), z)
            piece = cut(batch, start, size)

            @pl.when(target != 0)
            def _():
                pltpu.make_async_remote_copy(
                    src_ref=piece, dst_ref=piece, send_sem=st_s.at[batch, stage], recv_sem=st_r.at[batch, stage],
                    device_id=(h, target), device_id_type=MESH,
                ).start()

    def stage(batch, number):
        z_first = batches[batch][2]
        major, minor = (y, z) if z_first else (z, y)

        @pl.when(core == 0)
        def _():
            if number == 0:
                @pl.when(f != 0)
                def _():
                    arrived(cut(batch, 0, 32), sc_r.at[batch])

                peers_copy(batch, 0, pl.multiple_of((major * 4 + minor) * 32, 32), 32, z_first)
            elif number == 1:
                @pl.when(f != 0)
                def _():
                    arrived(cut(batch, 0, 96), st_r.at[batch, 0])

                peers_copy(batch, 1, pl.multiple_of(major * 128, 128), 128, not z_first)
            else:
                @pl.when(f != 0)
                def _():
                    arrived(cut(batch, 0, 384), st_r.at[batch, 1])

                piece = cut(batch, 0, TOK)
                pltpu.make_async_remote_copy(
                    src_ref=piece, dst_ref=piece, send_sem=st_s.at[batch, 2], recv_sem=st_r.at[batch, 2],
                    device_id=(h, f + 1), device_id_type=MESH,
                ).start()

    def stages_done(batch):
        @pl.when(core == 1)
        def _():
            arrived(cut(batch, 0, TOK), st_r.at[batch, 2])

    def stages_sent(batch):
        @pl.when(f == 0)
        def _():
            arrived(cut(batch, 0, 480), sc_s.at[batch])

        @pl.when(core == 0)
        def _():
            for number, size in ((0, 32), (1, 128)):
                along_z = batches[batch][2] == (number == 0)
                on_line = ((y == 0) & (z != 0)) if along_z else ((z == 0) & (y != 0))

                @pl.when(on_line)
                def _():
                    arrived(cut(batch, 0, 2 * size), st_s.at[batch, number])

                @pl.when(jnp.logical_not(on_line))
                def _():
                    arrived(cut(batch, 0, 3 * size), st_s.at[batch, number])

            arrived(cut(batch, 0, TOK), st_s.at[batch, 2])

    def send_wave(v):
        picked = jnp.concatenate(
            [qkv[j, WT * v : WT * v + WT, : 3 * HD] for j in range(HPG)], axis=0
        )
        sbuf[v] = dot(perm[...], picked).astype(BF)

        @pl.loop(1, nf)
        def _(i):
            p = lax.rem(f + i, nf)
            pltpu.make_async_remote_copy(
                src_ref=sbuf.at[v, pl.ds(pl.multiple_of(p * 16, 16), 16)],
                dst_ref=rbuf.at[v, pl.ds(pl.multiple_of(f * 16, 16), 16), pl.ds(0, 3 * HD)],
                send_sem=a2a_s.at[v], recv_sem=a2a_r.at[v], device_id=(h, p), device_id_type=MESH,
            ).start()

        own = pl.ds(pl.multiple_of(f * 16, 16), 16)
        rbuf[v, own, : 3 * HD] = sbuf[v, own]

    def attend(scores, vals):
        return dot(jnp.exp2(scores).astype(BF), vals)

    def close(total):
        return (total[:, :HD] / total[:, HD:]).astype(BF)

    def temporal(v):
        arrived(rbuf.at[v, pl.ds(0, 496), pl.ds(0, 3 * HD)], a2a_r.at[v])
        scores = dot_t(rbuf[v, :, :HD], rbuf[v, :, HD : 2 * HD])
        same = (lax.broadcasted_iota(jnp.int32, (TOK, TOK), 0) % 16) == (
            lax.broadcasted_iota(jnp.int32, (TOK, TOK), 1) % 16
        )
        weights = jnp.where(same, jnp.exp2(scores), 0.0).astype(BF)
        obuf[v] = close(dot(weights, rbuf[v, :, 2 * HD :]))

        @pl.loop(1, nf)
        def _(i):
            p = lax.rem(f + i, nf)
            pltpu.make_async_remote_copy(
                src_ref=obuf.at[v, pl.ds(pl.multiple_of(p * 16, 16), 16)],
                dst_ref=tbuf.at[v, pl.ds(pl.multiple_of(f * 16, 16), 16)],
                send_sem=ret_s.at[v], recv_sem=ret_r.at[v], device_id=(h, p), device_id_type=MESH,
            ).start()

        own = pl.ds(pl.multiple_of(f * 16, 16), 16)
        tbuf[v, own] = obuf[v, own]

    def spatial(j):
        query = qkv[j, :, :HD]
        total = attend(dot_t(query, qkv[j, :, HD : 2 * HD]), qkv[j, :, 2 * HD :])
        total = total + attend(dot_t(query, kv0[j, :, :HD]), kv0[j, :, HD:])
        sp[j] = close(total)

    def copy_to(src, dst, send_sem, recv_sem, peer):
        return pltpu.make_async_remote_copy(
            src_ref=src, dst_ref=dst, send_sem=send_sem, recv_sem=recv_sem,
            device_id=(peer, f), device_id_type=MESH,
        )

    def far_copies(v):
        return (
            copy_to(far_s.at[v, 0], far_r.at[v, 0], fs_sem.at[v, 0], fr_sem.at[v, 0], left),
            copy_to(far_s.at[v, 1], far_r.at[v, 1], fs_sem.at[v, 1], fr_sem.at[v, 1], right),
        )

    def near_copies(v):
        return (
            copy_to(near_s.at[v, 0], near_r.at[v, 0], ns_sem.at[v, 0], nr_sem.at[v, 0], left),
            copy_to(near_s.at[v, 1], near_r.at[v, 1], ns_sem.at[v, 1], nr_sem.at[v, 1], right),
        )

    def project_out(v):
        rows = slice(WT * v, WT * v + WT)
        arrived(tbuf.at[v, pl.ds(0, 496)], ret_r.at[v])
        back = dot(unperm[...], tbuf[v])
        for j in range(HPG):
            block = back[WT * j : WT * j + WT] + sp[j, rows].astype(F32) * (1.0 - kind[j])
            att[rows, HD * j : HD * j + HD] = block.astype(BF)
        part = dot(att[rows], wo[opposite]).astype(BF)
        far_s[v, 0] = part[:HALF]
        far_s[v, 1] = part[HALF:]
        for copy in far_copies(v):
            copy.start()

    def reduce_near(v):
        rows = slice(WT * v, WT * v + WT)
        far = far_copies(v)
        near = near_copies(v)
        part = dot(att[rows], wo[left])
        far[0].wait_recv()
        near_s[v, 0, :HALF] = (part[:HALF] + far_r[v, 0].astype(F32)).astype(BF)
        near_s[v, 0, HALF:] = part[HALF:].astype(BF)
        near[0].start()
        part = dot(att[rows], wo[right])
        far[1].wait_recv()
        near_s[v, 1, :HALF] = part[:HALF].astype(BF)
        near_s[v, 1, HALF:] = (part[HALF:] + far_r[v, 1].astype(F32)).astype(BF)
        near[1].start()

    def finish(v):
        rows = slice(WT * v, WT * v + WT)
        near = near_copies(v)
        part = dot(att[rows], wo[h]).astype(BF).astype(F32)
        near[0].wait_recv()
        near[1].wait_recv()
        out_ref[rows] = (part + near_r[v, 0].astype(F32) + near_r[v, 1].astype(F32)).astype(BF)

    loads[0].wait()
    project(0)
    pl.semaphore_wait(barrier, nf + 1)
    project(1)
    scatter(0)
    project(2)
    scatter(1)
    send_wave(0)
    stage(0, 0)
    send_wave(1)
    stage(0, 1)
    stage(1, 0)
    for b in range(4):
        loads[4 + b].wait()
    stage(0, 2)
    stage(1, 1)
    send_wave(2)
    stage(1, 2)
    temporal(0)
    send_wave(3)
    stages_done(0)
    stages_done(1)
    for j in range(HPG):
        spatial(j)
    project_out(0)
    temporal(1)
    reduce_near(0)
    project_out(1)
    temporal(2)
    reduce_near(1)
    project_out(2)
    temporal(3)
    reduce_near(2)
    finish(0)
    project_out(3)
    reduce_near(3)
    finish(1)
    finish(2)
    finish(3)

    stages_sent(0)
    stages_sent(1)
    for v in range(WAVES):
        arrived(sbuf.at[v, pl.ds(0, 496)], a2a_s.at[v])
        arrived(obuf.at[v, pl.ds(0, 496)], ret_s.at[v])
        for copy in far_copies(v) + near_copies(v):
            copy.wait_send()


def per_device(frames_x, w_qkv, q_gain, k_gain, head_kind, w_out):
    any_spec = pl.BlockSpec(memory_space=pl.ANY)
    vmem = pl.BlockSpec(memory_space=pltpu.VMEM)
    dma = pltpu.SemaphoreType.DMA
    return pl.pallas_call(
        kernel,
        out_shape=jax.ShapeDtypeStruct((TOK, COLS), BF),
        in_specs=[pl.BlockSpec(memory_space=pltpu.SMEM), any_spec, any_spec, vmem, vmem, any_spec],
        out_specs=vmem,
        scratch_shapes=[
            pltpu.VMEM((TOK, D), BF),
            pltpu.VMEM((3, D, 768), BF),
            pltpu.VMEM((4, HPG * HD, COLS), BF),
            pltpu.VMEM((HPG, TOK, 4 * HD), BF),
            pltpu.VMEM((HPG, TOK, 3 * HD), BF),
            pltpu.VMEM((WAVES, TOK, 3 * HD), BF),
            pltpu.VMEM((WAVES, TOK, 4 * HD), BF),
            pltpu.VMEM((WAVES, TOK, HD), BF),
            pltpu.VMEM((WAVES, TOK, HD), BF),
            pltpu.VMEM((TOK, HPG * WT), BF),
            pltpu.VMEM((HPG * WT, TOK), BF),
            pltpu.VMEM((HPG, TOK, HD), BF),
            pltpu.VMEM((TOK, HPG * HD), BF),
            pltpu.VMEM((WAVES, 2, HALF, COLS), BF),
            pltpu.VMEM((WAVES, 2, HALF, COLS), BF),
            pltpu.VMEM((WAVES, 2, WT, COLS), BF),
            pltpu.VMEM((WAVES, 2, WT, COLS), BF),
            dma((8,)),
            dma((WAVES,)),
            dma((WAVES,)),
            dma((WAVES,)),
            dma((WAVES,)),
            dma((2,)),
            dma((2,)),
            dma((2, 3)),
            dma((2, 3)),
            dma((WAVES, 2)),
            dma((WAVES, 2)),
            dma((WAVES, 2)),
            dma((WAVES, 2)),
        ],
        compiler_params=pltpu.CompilerParams(
            collective_id=0, has_side_effects=True, vmem_limit_bytes=60 * 1024 * 1024
        ),
    )(head_kind, frames_x, w_qkv, q_gain.reshape(1, HD), k_gain.reshape(1, HD), w_out)


def solution(mesh):
    placed = (P("frame", None), P(None, "head"), P(), P(), P("head"), P("head", None))
    return jax.shard_map(
        per_device, mesh=mesh, in_specs=placed, out_specs=P("frame", "head"), check_vma=False
    )
```

time: 377 us -> 95 us (0.25)
  waiting for transfers between devices: 224 us -> 0 us
  Pallas kernels: 0 us -> 92.8 us
  matrix products: 71.6 us -> 0 us
  local copies, waits for them, and re-layouts: 44.8 us -> 2.06 us
  other arithmetic: 22 us -> 0 us
  between operations: 13.3 us -> 0.01 us
    psum x1 -> x0, waiting for transfers between devices: 101 us -> none  [from_root(): return lax.psum(block, axis)]
    pallas_call x0 -> x1, Pallas kernels: none -> 92.8 us  [per_device(): pl.pallas_call(kernel, out_shape=jax.ShapeDtypeStruct((TOK, COLS), BF), i...]
    all_gather x1 -> x0, waiting for transfers between devices: 85.8 us -> none  [per_device(): lax.all_gather(temporal_in[:, :, head_dim:], 'frame', axis=1, tiled=True)]
    dot_general x8 -> x0, matrix products: 71.6 us -> none  [the longest x1 17.1 us: per_device(): jnp.einsum('stf,sftd->std', probs, remote[..., head_dim:], preferred_elem...]
    reduce_scatter x1 -> x0, waiting for transfers between devices: 37.6 us -> none  [per_device(): lax.psum_scatter(group_part.astype(jnp.bfloat16), 'head', scatter_dimensi...]
    slice x7 -> x0, local copies, waits for them, and re-layouts: 28.6 us -> none  [the longest x1 23.1 us: per_device(): remote[..., head_dim:]]
    sub x1 -> x0, other arithmetic: 10.8 us -> none  [softmax_rows(): shifted = scores - jnp.max(scores, axis=-1, keepdims=True)]
    unnamed x22 -> x1, local copies, waits for them, and re-layouts: 8.09 us -> 2.06 us
  transfers between devices with their start and end apart: 3 -> 0, of which waited for: 3 -> 0; matrix products, arithmetic and copies ran while one was open for 10% -> 0% of each run, Pallas kernels for 0% -> 0%
where the time goes in v1:
time: 95 us; the launch traced here: 94.9 us
  Pallas kernels  92.8 us (98%)
  local copies, waits for them, and re-layouts  2.06 us (2%)
    pallas_call x1, Pallas kernels, per_device(): pl.pallas_call(kernel, out_shape=jax.ShapeDtypeStruct((TOK, COLS), BF), i...  92.8 us
    unnamed x1, local copies, waits for them, and re-layouts  2.06 us

profile of v1, /device:TPU:0, one launch (start us, length us, event | category | flops | bytes accessed | tf_op | source)
XLA Modules:
  0.0 94.9 jit_solution(7968115549419264437)
XLA Ops:
  0.0 92.8 %shard_map.64 = bf16[512,768]{1,0:T(8,128)(2,1)} custom-call(s32[6]{0:T(128)} %kinds.1, bf16[512,3072]{1,0:T(8,128)(2,1)} %x_hbm.1, bf16[3072,2304]{1,0:T(8,128)(2,1)} %w_hbm.1, f32[1,128]{1,0:T(1,128)} %bitcast.2, f32[1,128]{1,0:T(1,128)} %bitcast.3, bf16[768,3072]{1,0:T(8,128)(2,1)} %wo_hbm.1), custom_call_target="tpu_custom_call" | custom-call | tf_op jit(solution)/shard_map/pallas_call | solution.py:381
  92.8 2.1 %copy.8 = bf16[512,768]{1,0:T(8,128)(2,1)} copy(bf16[512,768]{1,0:T(8,128)(2,1)} %shard_map.64) | data formatting | bytes 1572864

commit v2 on v1

v2 whole, which is shorter than its diff:
```python
import functools
import math

import jax
import jax.numpy as jnp
from jax import lax
from jax.experimental import pallas as pl
from jax.experimental.pallas import tpu as pltpu
from jax.sharding import PartitionSpec as P

MESH = pl.DeviceIdType.MESH
EPSILON = 1e-06
HPG = 6
TMAX = 4
HD = 128
TOK = 512
D = 3072
WAVES = 4
WT = TOK // WAVES
COLS = D // 4
CHUNKS = 9
SECTIONS = ((0,), (1, 2), (3, 4, 5), (6, 7, 8))
STARTS = (4, 6, 9, 12, 14)
HALF = WT // 2
WIDE = COLS // 2
BATCH = 2
BATCHES = HPG // BATCH
BF = jnp.bfloat16
F32 = jnp.float32


def dot(a, b):
    return jnp.dot(a, b, preferred_element_type=F32)


def dot_t(a, b):
    return lax.dot_general(a, b, (((1,), (1,)), ((), ())), preferred_element_type=F32)


def arrived(ref, sem):
    pltpu.make_async_copy(ref, ref, sem).wait()


def kernel(
    kinds, x_hbm, w_hbm, qg_ref, kg_ref, wo_hbm, out_ref,
    x, w, wo, raw, qkv, kv0, sbuf, rbuf, obuf, tbuf, perm, unperm, sp, att,
    far_s, far_r, near_s, near_r,
    load_sem, a2a_s, a2a_r, ret_s, ret_r, sc_s, sc_r, st_s, st_r, co_s, co_r, fs_sem, fr_sem, ns_sem, nr_sem,
):
    nf = 32
    h = lax.axis_index("head")
    f = lax.axis_index("frame")
    core = lax.rem(f, 2)
    chip = f // 2
    left, right, opposite = lax.rem(h + 3, 4), lax.rem(h + 1, 4), lax.rem(h + 2, 4)

    barrier = pltpu.get_barrier_semaphore()

    @pl.loop(1, nf)
    def _(i):
        pl.semaphore_signal(barrier, inc=1, device_id=(h, lax.rem(f + i, nf)), device_id_type=MESH)

    for peer in (left, right):
        pl.semaphore_signal(barrier, inc=1, device_id=(peer, f), device_id_type=MESH)

    loads = [pltpu.make_async_copy(x_hbm, x, load_sem.at[0])]
    for c in range(CHUNKS):
        loads.append(
            pltpu.make_async_copy(w_hbm.at[:, pl.ds(256 * c, 256)], w.at[c], load_sem.at[1 + c])
        )
    for b in range(4):
        loads.append(
            pltpu.make_async_copy(wo_hbm.at[:, pl.ds(COLS * b, COLS)], wo.at[b], load_sem.at[10 + b])
        )
    for load in loads[: STARTS[0]]:
        load.start()

    kind = [kinds[j] for j in range(HPG)]
    count = sum(kind)
    holds = [[None] * HPG for _ in range(TMAX)]
    before = jnp.int32(0)
    for j in range(HPG):
        rank = kind[j] * before + (1 - kind[j]) * (count + j - before)
        for t in range(TMAX):
            holds[t][j] = (1 - jnp.minimum((rank - t) * (rank - t), 1)).astype(F32)
        before = before + kind[j]
    kind = [val.astype(F32) for val in kind]

    def spread(shape, mixed_dim):
        mixed = lax.broadcasted_iota(jnp.int32, shape, mixed_dim)
        token = lax.broadcasted_iota(jnp.int32, shape, 1 - mixed_dim)
        same = ((mixed // 16) * 4 + mixed % 4 == token).astype(F32)
        slot = (mixed // 4) % 4
        return [jnp.where(slot == t, same, 0.0) for t in range(TMAX)]

    slots = spread((TOK, WT), 0)
    for j in range(HPG):
        perm[:, WT * j : WT * j + WT] = sum(slots[t] * holds[t][j] for t in range(TMAX)).astype(BF)
    slots = spread((WT, TOK), 1)
    for j in range(HPG):
        total = sum(slots[t] * (holds[t][j] * kind[j]) for t in range(TMAX))
        unperm[WT * j : WT * j + WT] = total.astype(BF)
    for j in range(HPG):
        qkv[j, :, 3 * HD :] = jnp.ones((TOK, HD), BF)
        kv0[j, :, 2 * HD :] = jnp.ones((TOK, HD), BF)
    for v in range(WAVES):
        rbuf[v, :, 3 * HD :] = jnp.ones((TOK, HD), BF)

    q_gain = qg_ref[...] * (math.log2(math.e) / math.sqrt(HD))
    k_gain = kg_ref[...]

    def norm(val, gain):
        mean_square = jnp.mean(val * val, axis=-1, keepdims=True)
        return (val * lax.rsqrt(mean_square + EPSILON) * gain).astype(BF)

    def project(number):
        for c in SECTIONS[number]:
            loads[1 + c].wait()
        for load in loads[STARTS[number] : STARTS[number + 1]]:
            load.start()
        for i, c in enumerate(SECTIONS[number]):
            raw[number % 2, :, 256 * i : 256 * i + 256] = dot(x[...], w[c])

    def settle(number):
        for piece in range(2 * SECTIONS[number][0], 2 * SECTIONS[number][-1] + 2):
            head, role = piece // 3, piece % 3
            at = HD * (piece - 2 * SECTIONS[number][0])
            block = raw[number % 2, :, at : at + HD]
            if role == 0:
                block = norm(block, q_gain)
            elif role == 1:
                block = norm(block, k_gain)
            else:
                block = block.astype(BF)
            qkv[head, :, HD * role : HD * role + HD] = block

    def cut(batch, start, size, own=False):
        heads = pl.ds(BATCH * batch, BATCH)
        if own:
            return qkv.at[heads, pl.ds(start, size), pl.ds(HD, 2 * HD)]
        return kv0.at[heads, pl.ds(start, size), pl.ds(0, 2 * HD)]

    def spread_copy(batch, start, size, own, send_sem, recv_sem, target):
        pltpu.make_async_remote_copy(
            src_ref=cut(batch, start, size, own), dst_ref=cut(batch, start, size),
            send_sem=send_sem, recv_sem=recv_sem, device_id=(h, target), device_id_type=MESH,
        ).start()

    def push(batch, own):
        mine = pl.multiple_of(chip * 32, 32)

        @pl.loop(1, 16)
        def _(i):
            target = lax.rem(chip + i, 16)

            @pl.when(target != 0)
            def _():
                spread_copy(batch, mine, 32, own, st_s.at[batch], st_r.at[batch], 2 * target)

    def hand_over(batch, own):
        spread_copy(batch, 0, TOK, own, co_s.at[batch], co_r.at[batch], f + 1)

    def root_scatter(batch):
        @pl.when(f == 0)
        def _():
            @pl.loop(1, 16)
            def _(q):
                spread_copy(batch, pl.multiple_of(q * 32, 32), 32, True, sc_s.at[batch], sc_r.at[batch], 2 * q)

    def root_push():
        @pl.when(f == 0)
        def _():
            for batch in range(BATCHES):
                push(batch, True)
                hand_over(batch, True)
            for j in range(HPG):
                kv0[j, :, : 2 * HD] = qkv[j, :, HD : 3 * HD]

    def relay(batch):
        @pl.when((core == 0) & (f != 0))
        def _():
            arrived(cut(batch, 0, 32), sc_r.at[batch])
            push(batch, False)

    def collect(batch):
        @pl.when((core == 0) & (f != 0))
        def _():
            arrived(cut(batch, 0, 480), st_r.at[batch])
            hand_over(batch, False)

    def first_here(batch):
        @pl.when(core == 1)
        def _():
            arrived(cut(batch, 0, TOK), co_r.at[batch])

    def spread_sent(batch):
        @pl.when(f == 0)
        def _():
            arrived(cut(batch, 0, 480), sc_s.at[batch])
            arrived(cut(batch, 0, 480), st_s.at[batch])
            arrived(cut(batch, 0, TOK), co_s.at[batch])

        @pl.when((core == 0) & (f != 0))
        def _():
            arrived(cut(batch, 0, 448), st_s.at[batch])
            arrived(cut(batch, 0, TOK), co_s.at[batch])

    def send_wave(v):
        picked = jnp.concatenate(
            [qkv[j, WT * v : WT * v + WT, : 3 * HD] for j in range(HPG)], axis=0
        )
        sbuf[v] = dot(perm[...], picked).astype(BF)

        @pl.loop(1, nf)
        def _(i):
            p = lax.rem(f + i, nf)
            pltpu.make_async_remote_copy(
                src_ref=sbuf.at[v, pl.ds(pl.multiple_of(p * 16, 16), 16)],
                dst_ref=rbuf.at[v, pl.ds(pl.multiple_of(f * 16, 16), 16), pl.ds(0, 3 * HD)],
                send_sem=a2a_s.at[v], recv_sem=a2a_r.at[v], device_id=(h, p), device_id_type=MESH,
            ).start()

        own = pl.ds(pl.multiple_of(f * 16, 16), 16)
        rbuf[v, own, : 3 * HD] = sbuf[v, own]

    def attend(scores, vals):
        return dot(jnp.exp2(scores).astype(BF), vals)

    def close(total):
        return (total[:, :HD] / total[:, HD:]).astype(BF)

    def temporal(v):
        arrived(rbuf.at[v, pl.ds(0, 496), pl.ds(0, 3 * HD)], a2a_r.at[v])
        scores = dot_t(rbuf[v, :, :HD], rbuf[v, :, HD : 2 * HD])
        same = (lax.broadcasted_iota(jnp.int32, (TOK, TOK), 0) % 16) == (
            lax.broadcasted_iota(jnp.int32, (TOK, TOK), 1) % 16
        )
        weights = jnp.where(same, jnp.exp2(scores), 0.0).astype(BF)
        obuf[v] = close(dot(weights, rbuf[v, :, 2 * HD :]))

        @pl.loop(1, nf)
        def _(i):
            p = lax.rem(f + i, nf)
            pltpu.make_async_remote_copy(
                src_ref=obuf.at[v, pl.ds(pl.multiple_of(p * 16, 16), 16)],
                dst_ref=tbuf.at[v, pl.ds(pl.multiple_of(f * 16, 16), 16)],
                send_sem=ret_s.at[v], recv_sem=ret_r.at[v], device_id=(h, p), device_id_type=MESH,
            ).start()

        own = pl.ds(pl.multiple_of(f * 16, 16), 16)
        tbuf[v, own] = obuf[v, own]

    def spatial_own(j):
        at = slice(2 * HD * (j % 3), 2 * HD * (j % 3) + 2 * HD)
        raw[j // 3, :, at] = attend(dot_t(qkv[j, :, :HD], qkv[j, :, HD : 2 * HD]), qkv[j, :, 2 * HD :])

    def spatial_first(j):
        at = slice(2 * HD * (j % 3), 2 * HD * (j % 3) + 2 * HD)
        total = attend(dot_t(qkv[j, :, :HD], kv0[j, :, :HD]), kv0[j, :, HD:])
        sp[j] = close(raw[j // 3, :, at] + total)

    def copy_to(src, dst, send_sem, recv_sem, peer):
        return pltpu.make_async_remote_copy(
            src_ref=src, dst_ref=dst, send_sem=send_sem, recv_sem=recv_sem,
            device_id=(peer, f), device_id_type=MESH,
        )

    def far_copies(v):
        return [
            copy_to(
                far_s.at[v, side, :, pl.ds(WIDE * part, WIDE)], far_r.at[v, side, :, pl.ds(WIDE * part, WIDE)],
                fs_sem.at[v, side, part], fr_sem.at[v, side, part], (left, right)[side],
            )
            for part in range(2) for side in range(2)
        ]

    def near_copies(v):
        return [
            copy_to(
                near_s.at[v, side, :, pl.ds(WIDE * part, WIDE)], near_r.at[v, side, :, pl.ds(WIDE * part, WIDE)],
                ns_sem.at[v, side, part], nr_sem.at[v, side, part], (left, right)[side],
            )
            for part in range(2) for side in range(2)
        ]

    def project_out(v):
        rows = slice(WT * v, WT * v + WT)
        arrived(tbuf.at[v, pl.ds(0, 496)], ret_r.at[v])
        back = dot(unperm[...], tbuf[v])
        for j in range(HPG):
            block = back[WT * j : WT * j + WT] + sp[j, rows].astype(F32) * (1.0 - kind[j])
            att[rows, HD * j : HD * j + HD] = block.astype(BF)
        part = dot(att[rows], wo[opposite]).astype(BF)
        far_s[v, 0] = part[:HALF]
        far_s[v, 1] = part[HALF:]
        for copy in far_copies(v):
            copy.start()

    def near_terms(v):
        rows = slice(WT * v, WT * v + WT)
        near_s[v, 0] = dot(att[rows], wo[left]).astype(BF)
        near_s[v, 1] = dot(att[rows], wo[right]).astype(BF)

    def reduce_near(v):
        far = far_copies(v)
        near = near_copies(v)
        for part in range(2):
            cols = slice(WIDE * part, WIDE * part + WIDE)
            for side in range(2):
                rows = slice(HALF * side, HALF * side + HALF)
                far[2 * part + side].wait_recv()
                total = near_s[v, side, rows, cols].astype(F32) + far_r[v, side, :, cols].astype(F32)
                near_s[v, side, rows, cols] = total.astype(BF)
                near[2 * part + side].start()

    def finish(v):
        rows = slice(WT * v, WT * v + WT)
        part = dot(att[rows], wo[h]).astype(BF).astype(F32)
        for copy in near_copies(v):
            copy.wait_recv()
        out_ref[rows] = (part + near_r[v, 0].astype(F32) + near_r[v, 1].astype(F32)).astype(BF)

    loads[0].wait()
    project(0)
    project(1)
    settle(0)
    project(2)
    settle(1)
    pl.semaphore_wait(barrier, nf + 1)
    root_scatter(0)
    relay(0)
    project(3)
    settle(2)
    root_scatter(1)
    relay(1)
    settle(3)
    root_scatter(2)
    root_push()
    relay(2)
    send_wave(0)
    send_wave(1)
    for j in range(HPG):
        spatial_own(j)
    collect(0)
    collect(1)
    collect(2)
    for b in range(4):
        loads[10 + b].wait()
    send_wave(2)
    temporal(0)
    for batch in range(BATCHES):
        first_here(batch)
    for j in range(HPG):
        spatial_first(j)
    send_wave(3)
    project_out(0)
    near_terms(0)
    temporal(1)
    reduce_near(0)
    project_out(1)
    near_terms(1)
    temporal(2)
    reduce_near(1)
    project_out(2)
    near_terms(2)
    temporal(3)
    finish(0)
    reduce_near(2)
    project_out(3)
    near_terms(3)
    finish(1)
    reduce_near(3)
    finish(2)
    finish(3)

    for batch in range(BATCHES):
        spread_sent(batch)
    for v in range(WAVES):
        arrived(sbuf.at[v, pl.ds(0, 496)], a2a_s.at[v])
        arrived(obuf.at[v, pl.ds(0, 496)], ret_s.at[v])
        for copy in far_copies(v) + near_copies(v):
            copy.wait_send()


def per_device(frames_x, w_qkv, q_gain, k_gain, head_kind, w_out):
    any_spec = pl.BlockSpec(memory_space=pl.ANY)
    vmem = pl.BlockSpec(memory_space=pltpu.VMEM)
    dma = pltpu.SemaphoreType.DMA
    return pl.pallas_call(
        kernel,
        out_shape=jax.ShapeDtypeStruct((TOK, COLS), BF),
        in_specs=[pl.BlockSpec(memory_space=pltpu.SMEM), any_spec, any_spec, vmem, vmem, any_spec],
        out_specs=vmem,
        scratch_shapes=[
            pltpu.VMEM((TOK, D), BF),
            pltpu.VMEM((CHUNKS, D, 256), BF),
            pltpu.VMEM((4, HPG * HD, COLS), BF),
            pltpu.VMEM((2, TOK, 768), F32),
            pltpu.VMEM((HPG, TOK, 4 * HD), BF),
            pltpu.VMEM((HPG, TOK, 3 * HD), BF),
            pltpu.VMEM((WAVES, TOK, 3 * HD), BF),
            pltpu.VMEM((WAVES, TOK, 4 * HD), BF),
            pltpu.VMEM((WAVES, TOK, HD), BF),
            pltpu.VMEM((WAVES, TOK, HD), BF),
            pltpu.VMEM((TOK, HPG * WT), BF),
            pltpu.VMEM((HPG * WT, TOK), BF),
            pltpu.VMEM((HPG, TOK, HD), BF),
            pltpu.VMEM((TOK, HPG * HD), BF),
            pltpu.VMEM((WAVES, 2, HALF, COLS), BF),
            pltpu.VMEM((WAVES, 2, HALF, COLS), BF),
            pltpu.VMEM((WAVES, 2, WT, COLS), BF),
            pltpu.VMEM((WAVES, 2, WT, COLS), BF),
            dma((14,)),
            dma((WAVES,)),
            dma((WAVES,)),
            dma((WAVES,)),
            dma((WAVES,)),
            dma((BATCHES,)),
            dma((BATCHES,)),
            dma((BATCHES,)),
            dma((BATCHES,)),
            dma((BATCHES,)),
            dma((BATCHES,)),
            dma((WAVES, 2, 2)),
            dma((WAVES, 2, 2)),
            dma((WAVES, 2, 2)),
            dma((WAVES, 2, 2)),
        ],
        compiler_params=pltpu.CompilerParams(
            collective_id=0, has_side_effects=True, vmem_limit_bytes=60 * 1024 * 1024
        ),
    )(head_kind, frames_x, w_qkv, q_gain.reshape(1, HD), k_gain.reshape(1, HD), w_out)


def solution(mesh):
    placed = (P("frame", None), P(None, "head"), P(), P(), P("head"), P("head", None))
    return jax.shard_map(
        per_device, mesh=mesh, in_specs=placed, out_specs=P("frame", "head"), check_vma=False
    )
```

time: 95 us -> 83.8 us (0.88)
  Pallas kernels: 92.8 us -> 81.6 us
    pallas_call x1, Pallas kernels: 92.8 us -> 81.6 us  [per_device(): pl.pallas_call(kernel, out_shape=jax.ShapeDtypeStruct((TOK, COLS), BF), i...]
where the time goes in v2:
time: 83.8 us; the launch traced here: 83.7 us
  Pallas kernels  81.6 us (97%)
  local copies, waits for them, and re-layouts  2.06 us (2%)
    pallas_call x1, Pallas kernels, per_device(): pl.pallas_call(kernel, out_shape=jax.ShapeDtypeStruct((TOK, COLS), BF), i...  81.6 us
    unnamed x1, local copies, waits for them, and re-layouts  2.06 us

profile of v2, /device:TPU:0, one launch (start us, length us, event | category | flops | bytes accessed | tf_op | source)
XLA Modules:
  0.0 83.7 jit_solution(10762776169131109025)
XLA Ops:
  0.0 81.6 %shard_map.64 = bf16[512,768]{1,0:T(8,128)(2,1)} custom-call(s32[6]{0:T(128)} %kinds.1, bf16[512,3072]{1,0:T(8,128)(2,1)} %x_hbm.1, bf16[3072,2304]{1,0:T(8,128)(2,1)} %w_hbm.1, f32[1,128]{1,0:T(1,128)} %bitcast.2, f32[1,128]{1,0:T(1,128)} %bitcast.3, bf16[768,3072]{1,0:T(8,128)(2,1)} %wo_hbm.1), custom_call_target="tpu_custom_call" | custom-call | tf_op jit(solution)/shard_map/pallas_call | solution.py:389
  81.6 2.1 %copy.8 = bf16[512,768]{1,0:T(8,128)(2,1)} copy(bf16[512,768]{1,0:T(8,128)(2,1)} %shard_map.64) | data formatting | bytes 1572864

commit v3 on v2

--- a/solution.py
+++ b/solution.py
@@ -19,8 +19,9 @@
 WT = TOK // WAVES
 COLS = D // 4
 CHUNKS = 9
-SECTIONS = ((0,), (1, 2), (3, 4, 5), (6, 7, 8))
-STARTS = (4, 6, 9, 12, 14)
+SECTIONS = ((0, 1), (2, 3, 4, 5), (6, 7, 8))
+STARTS = (5, 13, 17, 17)
+WAITS = (0, 3, 7, 13)
 HALF = WT // 2
 WIDE = COLS // 2
 BATCH = 2
@@ -52,6 +53,7 @@
     f = lax.axis_index("frame")
     core = lax.rem(f, 2)
     chip = f // 2
+    y, z = chip // 4, lax.rem(chip, 4)
     left, right, opposite = lax.rem(h + 3, 4), lax.rem(h + 1, 4), lax.rem(h + 2, 4)
 
     barrier = pltpu.get_barrier_semaphore()
@@ -63,15 +65,19 @@
     for peer in (left, right):
         pl.semaphore_signal(barrier, inc=1, device_id=(peer, f), device_id_type=MESH)
 
-    loads = [pltpu.make_async_copy(x_hbm, x, load_sem.at[0])]
-    for c in range(CHUNKS):
-        loads.append(
-            pltpu.make_async_copy(w_hbm.at[:, pl.ds(256 * c, 256)], w.at[c], load_sem.at[1 + c])
+    sources = [(x_hbm, x)]
+    for j in range(HPG):
+        sources.append((w_hbm.at[:, pl.ds(3 * HD * j + HD, 2 * HD)], w.at[j]))
+    for j in range(HPG):
+        sources.append(
+            (w_hbm.at[:, pl.ds(3 * HD * j, HD)], w.at[HPG + j // 2, :, pl.ds(HD * (j % 2), HD)])
         )
     for b in range(4):
-        loads.append(
-            pltpu.make_async_copy(wo_hbm.at[:, pl.ds(COLS * b, COLS)], wo.at[b], load_sem.at[10 + b])
-        )
+        sources.append((wo_hbm.at[:, pl.ds(COLS * b, COLS)], wo.at[b]))
+    loads = [
+        pltpu.make_async_copy(source, target, load_sem.at[i])
+        for i, (source, target) in enumerate(sources)
+    ]
     for load in loads[: STARTS[0]]:
         load.start()
 
@@ -114,96 +120,118 @@
         return (val * lax.rsqrt(mean_square + EPSILON) * gain).astype(BF)
 
     def project(number):
-        for c in SECTIONS[number]:
-            loads[1 + c].wait()
+        for load in loads[WAITS[number] : WAITS[number + 1]]:
+            load.wait()
         for load in loads[STARTS[number] : STARTS[number + 1]]:
             load.start()
-        for i, c in enumerate(SECTIONS[number]):
-            raw[number % 2, :, 256 * i : 256 * i + 256] = dot(x[...], w[c])
-
-    def settle(number):
-        for piece in range(2 * SECTIONS[number][0], 2 * SECTIONS[number][-1] + 2):
-            head, role = piece // 3, piece % 3
-            at = HD * (piece - 2 * SECTIONS[number][0])
-            block = raw[number % 2, :, at : at + HD]
-            if role == 0:
-                block = norm(block, q_gain)
-            elif role == 1:
-                block = norm(block, k_gain)
+        for c in SECTIONS[number]:
+            val = dot(x[...], w[c])
+            one, two = val[:, :HD], val[:, HD:]
+            if c < HPG:
+                qkv[c, :, HD : 2 * HD] = norm(one, k_gain)
+                qkv[c, :, 2 * HD : 3 * HD] = two.astype(BF)
             else:
-                block = block.astype(BF)
-            qkv[head, :, HD * role : HD * role + HD] = block
-
-    def cut(batch, start, size, own=False):
-        heads = pl.ds(BATCH * batch, BATCH)
+                qkv[2 * (c - HPG), :, :HD] = norm(one, q_gain)
+                qkv[2 * (c - HPG) + 1, :, :HD] = norm(two, q_gain)
+
+    def cut(head, n, start, size, own=False):
+        heads = pl.ds(head, n)
         if own:
             return qkv.at[heads, pl.ds(start, size), pl.ds(HD, 2 * HD)]
         return kv0.at[heads, pl.ds(start, size), pl.ds(0, 2 * HD)]
 
-    def spread_copy(batch, start, size, own, send_sem, recv_sem, target):
+    def spread_copy(head, n, start, size, own, send_sem, recv_sem, target):
         pltpu.make_async_remote_copy(
-            src_ref=cut(batch, start, size, own), dst_ref=cut(batch, start, size),
+            src_ref=cut(head, n, start, size, own), dst_ref=cut(head, n, start, size),
             send_sem=send_sem, recv_sem=recv_sem, device_id=(h, target), device_id_type=MESH,
         ).start()
 
-    def push(batch, own):
-        mine = pl.multiple_of(chip * 32, 32)
-
-        @pl.loop(1, 16)
-        def _(i):
-            target = lax.rem(chip + i, 16)
-
-            @pl.when(target != 0)
-            def _():
-                spread_copy(batch, mine, 32, own, st_s.at[batch], st_r.at[batch], 2 * target)
+    def push(batch, number, own):
+        for side in range(2):
+            major, minor = ((y, z), (z, y))[side]
+            if number == 0:
+                start, size = pl.multiple_of((major * 4 + minor) * 32, 32), 32
+            else:
+                start, size = pl.multiple_of(major * 128, 128), 128
+            for i in range(1, 4):
+                if side == number:
+                    target = (y * 4 + lax.rem(z + i, 4)) * 2
+                else:
+                    target = (lax.rem(y + i, 4) * 4 + z) * 2
+
+                @pl.when(target != 0)
+                def _():
+                    spread_copy(
+                        BATCH * batch + side, 1, start, size, own,
+                        st_s.at[batch, number], st_r.at[batch, number], target,
+                    )
 
     def hand_over(batch, own):
-        spread_copy(batch, 0, TOK, own, co_s.at[batch], co_r.at[batch], f + 1)
+        spread_copy(BATCH * batch, BATCH, 0, TOK, own, co_s.at[batch], co_r.at[batch], f + 1)
 
     def root_scatter(batch):
         @pl.when(f == 0)
         def _():
             @pl.loop(1, 16)
             def _(q):
-                spread_copy(batch, pl.multiple_of(q * 32, 32), 32, True, sc_s.at[batch], sc_r.at[batch], 2 * q)
+                start = pl.multiple_of(q * 32, 32)
+                for side in range(2):
+                    target = 2 * q if side == 0 else (lax.rem(q, 4) * 4 + q // 4) * 2
+                    spread_copy(BATCH * batch + side, 1, start, 32, True, sc_s.at[batch], sc_r.at[batch], target)
 
     def root_push():
         @pl.when(f == 0)
         def _():
             for batch in range(BATCHES):
-                push(batch, True)
+                push(batch, 0, True)
+                push(batch, 1, True)
                 hand_over(batch, True)
             for j in range(HPG):
                 kv0[j, :, : 2 * HD] = qkv[j, :, HD : 3 * HD]
 
-    def relay(batch):
+    def whole(batch, size):
+        return cut(BATCH * batch, BATCH, 0, size)
+
+    def relay(batch, number):
         @pl.when((core == 0) & (f != 0))
         def _():
-            arrived(cut(batch, 0, 32), sc_r.at[batch])
-            push(batch, False)
+            if number == 0:
+                arrived(whole(batch, 32), sc_r.at[batch])
+            else:
+                arrived(whole(batch, 96), st_r.at[batch, 0])
+            push(batch, number, False)
 
     def collect(batch):
         @pl.when((core == 0) & (f != 0))
         def _():
-            arrived(cut(batch, 0, 480), st_r.at[batch])
+            arrived(whole(batch, 384), st_r.at[batch, 1])
             hand_over(batch, False)
 
     def first_here(batch):
         @pl.when(core == 1)
         def _():
-            arrived(cut(batch, 0, TOK), co_r.at[batch])
+            arrived(whole(batch, TOK), co_r.at[batch])
 
     def spread_sent(batch):
+        on_line = (chip != 0) & ((y == 0) | (z == 0))
+
         @pl.when(f == 0)
         def _():
-            arrived(cut(batch, 0, 480), sc_s.at[batch])
-            arrived(cut(batch, 0, 480), st_s.at[batch])
-            arrived(cut(batch, 0, TOK), co_s.at[batch])
-
-        @pl.when((core == 0) & (f != 0))
-        def _():
-            arrived(cut(batch, 0, 448), st_s.at[batch])
-            arrived(cut(batch, 0, TOK), co_s.at[batch])
+            arrived(whole(batch, 480), sc_s.at[batch])
+
+        @pl.when((core == 0) & on_line)
+        def _():
+            arrived(whole(batch, 80), st_s.at[batch, 0])
+            arrived(whole(batch, 320), st_s.at[batch, 1])
+
+        @pl.when((core == 0) & jnp.logical_not(on_line))
+        def _():
+            arrived(whole(batch, 96), st_s.at[batch, 0])
+            arrived(whole(batch, 384), st_s.at[batch, 1])
+
+        @pl.when(core == 0)
+        def _():
+            arrived(whole(batch, TOK), co_s.at[batch])
 
     def send_wave(v):
         picked = jnp.concatenate(
@@ -320,46 +348,44 @@
             copy.wait_recv()
         out_ref[rows] = (part + near_r[v, 0].astype(F32) + near_r[v, 1].astype(F32)).astype(BF)
 
-    loads[0].wait()
     project(0)
     project(1)
-    settle(0)
+    pl.semaphore_wait(barrier, nf + 1)
+    for batch in range(BATCHES):
+        root_scatter(batch)
+    root_push()
+    relay(0, 0)
     project(2)
-    settle(1)
-    pl.semaphore_wait(barrier, nf + 1)
-    root_scatter(0)
-    relay(0)
-    project(3)
-    settle(2)
-    root_scatter(1)
-    relay(1)
-    settle(3)
-    root_scatter(2)
-    root_push()
-    relay(2)
+    relay(1, 0)
+    relay(0, 1)
+    relay(2, 0)
     send_wave(0)
-    send_wave(1)
-    for j in range(HPG):
+    for j in range(3):
+        spatial_own(j)
+    relay(1, 1)
+    relay(2, 1)
+    for j in range(3, HPG):
         spatial_own(j)
     collect(0)
+    temporal(0)
     collect(1)
     collect(2)
+    send_wave(1)
     for b in range(4):
-        loads[10 + b].wait()
-    send_wave(2)
-    temporal(0)
+        loads[13 + b].wait()
     for batch in range(BATCHES):
         first_here(batch)
-    for j in range(HPG):
-        spatial_first(j)
-    send_wave(3)
+        for j in range(BATCH * batch, BATCH * batch + BATCH):
+            spatial_first(j)
     project_out(0)
     near_terms(0)
     temporal(1)
+    send_wave(2)
     reduce_near(0)
     project_out(1)
     near_terms(1)
     temporal(2)
+    send_wave(3)
     reduce_near(1)
     project_out(2)
     near_terms(2)
@@ -410,15 +436,15 @@
             pltpu.VMEM((WAVES, 2, HALF, COLS), BF),
             pltpu.VMEM((WAVES, 2, WT, COLS), BF),
             pltpu.VMEM((WAVES, 2, WT, COLS), BF),
-            dma((14,)),
+            dma((17,)),
             dma((WAVES,)),
             dma((WAVES,)),
             dma((WAVES,)),
             dma((WAVES,)),
             dma((BATCHES,)),
             dma((BATCHES,)),
-            dma((BATCHES,)),
-            dma((BATCHES,)),
+            dma((BATCHES, 2)),
+            dma((BATCHES, 2)),
             dma((BATCHES,)),
             dma((BATCHES,)),
             dma((WAVES, 2, 2)),

time: 83.8 us -> 81.8 us (0.976)
  Pallas kernels: 81.6 us -> 79.6 us
    pallas_call x1, Pallas kernels: 81.6 us -> 79.6 us  [per_device(): pl.pallas_call(kernel, out_shape=jax.ShapeDtypeStruct((TOK, COLS), BF), i...]
where the time goes in v3:
time: 81.8 us; the launch traced here: 81.7 us
  Pallas kernels  79.6 us (97%)
  local copies, waits for them, and re-layouts  2.06 us (3%)
    pallas_call x1, Pallas kernels, per_device(): pl.pallas_call(kernel, out_shape=jax.ShapeDtypeStruct((TOK, COLS), BF), i...  79.6 us
    unnamed x1, local copies, waits for them, and re-layouts  2.06 us

profile of v3, /device:TPU:0, one launch (start us, length us, event | category | flops | bytes accessed | tf_op | source)
XLA Modules:
  0.0 81.7 jit_solution(4029439581812420540)
XLA Ops:
  0.0 79.6 %shard_map.64 = bf16[512,768]{1,0:T(8,128)(2,1)} custom-call(s32[6]{0:T(128)} %kinds.1, bf16[512,3072]{1,0:T(8,128)(2,1)} %x_hbm.1, bf16[3072,2304]{1,0:T(8,128)(2,1)} %w_hbm.1, f32[1,128]{1,0:T(1,128)} %bitcast.2, f32[1,128]{1,0:T(1,128)} %bitcast.3, bf16[768,3072]{1,0:T(8,128)(2,1)} %wo_hbm.1), custom_call_target="tpu_custom_call" | custom-call | tf_op jit(solution)/shard_map/pallas_call | solution.py:415
  79.6 2.1 %copy.8 = bf16[512,768]{1,0:T(8,128)(2,1)} copy(bf16[512,768]{1,0:T(8,128)(2,1)} %shard_map.64) | data formatting | bytes 1572864

commit v4 on v3

--- a/solution.py
+++ b/solution.py
@@ -43,10 +43,10 @@
 
 
 def kernel(
-    kinds, x_hbm, w_hbm, qg_ref, kg_ref, wo_hbm, out_ref,
+    kinds, x_hbm, w_hbm, qg_ref, kg_ref, wo_hbm, out_hbm,
     x, w, wo, raw, qkv, kv0, sbuf, rbuf, obuf, tbuf, perm, unperm, sp, att,
-    far_s, far_r, near_s, near_r,
-    load_sem, a2a_s, a2a_r, ret_s, ret_r, sc_s, sc_r, st_s, st_r, co_s, co_r, fs_sem, fr_sem, ns_sem, nr_sem,
+    far_s, far_r, near_s, near_r, out_ref,
+    load_sem, a2a_s, a2a_r, ret_s, ret_r, sc_s, sc_r, st_s, st_r, co_s, co_r, fs_sem, fr_sem, ns_sem, nr_sem, out_sem,
 ):
     nf = 32
     h = lax.axis_index("head")
@@ -341,12 +341,17 @@
                 near_s[v, side, rows, cols] = total.astype(BF)
                 near[2 * part + side].start()
 
+    def out_copy(v):
+        rows = pl.ds(WT * v, WT)
+        return pltpu.make_async_copy(out_ref.at[rows], out_hbm.at[rows], out_sem.at[v])
+
     def finish(v):
         rows = slice(WT * v, WT * v + WT)
         part = dot(att[rows], wo[h]).astype(BF).astype(F32)
         for copy in near_copies(v):
             copy.wait_recv()
         out_ref[rows] = (part + near_r[v, 0].astype(F32) + near_r[v, 1].astype(F32)).astype(BF)
+        out_copy(v).start()
 
     project(0)
     project(1)
@@ -402,6 +407,7 @@
     for batch in range(BATCHES):
         spread_sent(batch)
     for v in range(WAVES):
+        out_copy(v).wait()
         arrived(sbuf.at[v, pl.ds(0, 496)], a2a_s.at[v])
         arrived(obuf.at[v, pl.ds(0, 496)], ret_s.at[v])
         for copy in far_copies(v) + near_copies(v):
@@ -416,7 +422,7 @@
         kernel,
         out_shape=jax.ShapeDtypeStruct((TOK, COLS), BF),
         in_specs=[pl.BlockSpec(memory_space=pltpu.SMEM), any_spec, any_spec, vmem, vmem, any_spec],
-        out_specs=vmem,
+        out_specs=any_spec,
         scratch_shapes=[
             pltpu.VMEM((TOK, D), BF),
             pltpu.VMEM((CHUNKS, D, 256), BF),
@@ -436,6 +442,7 @@
             pltpu.VMEM((WAVES, 2, HALF, COLS), BF),
             pltpu.VMEM((WAVES, 2, WT, COLS), BF),
             pltpu.VMEM((WAVES, 2, WT, COLS), BF),
+            pltpu.VMEM((TOK, COLS), BF),
             dma((17,)),
             dma((WAVES,)),
             dma((WAVES,)),
@@ -451,6 +458,7 @@
             dma((WAVES, 2, 2)),
             dma((WAVES, 2, 2)),
             dma((WAVES, 2, 2)),
+            dma((WAVES,)),
         ],
         compiler_params=pltpu.CompilerParams(
             collective_id=0, has_side_effects=True, vmem_limit_bytes=60 * 1024 * 1024

time: 81.8 us -> 81.6 us (level)
  no operation moved by 1% of the time
where the time goes in v4:
time: 81.6 us; the launch traced here: 81.4 us
  Pallas kernels  79.4 us (97%)
  local copies, waits for them, and re-layouts  2.06 us (3%)
    pallas_call x1, Pallas kernels, per_device(): pl.pallas_call(kernel, out_shape=jax.ShapeDtypeStruct((TOK, COLS), BF), i...  79.4 us
    unnamed x1, local copies, waits for them, and re-layouts  2.06 us

profile of v4, /device:TPU:0, one launch (start us, length us, event | category | flops | bytes accessed | tf_op | source)
XLA Modules:
  0.0 81.4 jit_solution(15401671304001842413)
XLA Ops:
  0.0 79.4 %shard_map.64 = bf16[512,768]{1,0:T(8,128)(2,1)} custom-call(s32[6]{0:T(128)} %kinds.1, bf16[512,3072]{1,0:T(8,128)(2,1)} %x_hbm.1, bf16[3072,2304]{1,0:T(8,128)(2,1)} %w_hbm.1, f32[1,128]{1,0:T(1,128)} %bitcast.2, f32[1,128]{1,0:T(1,128)} %bitcast.3, bf16[768,3072]{1,0:T(8,128)(2,1)} %wo_hbm.1), custom_call_target="tpu_custom_call" | custom-call | tf_op jit(solution)/shard_map/pallas_call | solution.py:421
  79.4 2.1 %copy.8 = bf16[512,768]{1,0:T(8,128)(2,1)} copy(bf16[512,768]{1,0:T(8,128)(2,1)} %shard_map.64) | data formatting | bytes 1572864
